TPU v7x, 256 devices: a whole 4x4x8 slice. The times are simulated.
256 devices in a mesh: tile: 64 (over x, z, core), pos: 4 (over y).
Axes of the slice: x: 4, y: 4, z: 8, core: 2. Of those that a mesh axis runs over, the one named last changes fastest.
Arguments:
- obj_real: float32 [4, 16384, 256], P(None, ('tile', 'pos')), may hold values from 0.5 to 1.5
- obj_imag: float32 [4, 16384, 256], P(None, ('tile', 'pos')), may hold values from -4 to 4
- probe: float32 [2, 128, 128], replicated, may hold values from -6 to 6
- fresnel_phase: float32 [33], replicated, may hold values from -3.140625 to 3.140625
- row_offset: int32 [4096], P('tile'), may hold values from 0 to 255
- col_offset: int32 [4096], P('tile'), may hold values from 0 to 128
- live_count: int32 [64], P('tile'), may hold values from 16 to 64, as said below
- measured: bfloat16 [4096, 128, 128], P('tile'), may hold values from 0.19921875 to 2
Outputs:
- grad_real: float32 [4, 16384, 256], P(None, ('tile', 'pos'))
- grad_imag: float32 [4, 16384, 256], P(None, ('tile', 'pos'))
Inputs may be any that keep to these rules, and one draw needn't show every extreme that they name: `row_offset`: row offsets count from the first of the 256 rows of the position's band. Band g uses its first live_count[g] slots; some band uses all 64.
All inputs are finite; a program needn't handle non-finite values.
Results may differ from a plain program's by a relative error of at most 0.012.
The roundings to bfloat16 on the way count: a program that leaves them out, or rounds other values in their place, can miss the bound.
Values sent between devices are 32-bit elements; how exact they have to be, the bound alone decides.
No kernel may reach another device: no remote copies, remote signals or barrier semaphores. Data moves between devices by JAX's collectives and lax.ppermute only.
A program may use at most 64 MiB of HBM per device.

v0:
```python
import jax
import jax.numpy as jnp
from jax import lax
from jax.sharding import PartitionSpec as P

AMP_FLOOR = 0.25


def from_behind(value, axis, steps):
    count = lax.axis_size(axis)
    leading, last = (max(0, -steps), min(count, count - steps))
    return lax.ppermute(value, axis, [(source, source + steps) for source in range(leading, last)])


def half_dot(left, right):
    return jnp.dot(
        left.astype(jnp.bfloat16), right.astype(jnp.bfloat16), preferred_element_type=jnp.float32
    )


def complex_dot(left, right):
    real = half_dot(left[0], right[0]) - half_dot(left[1], right[1])
    imag = half_dot(left[0], right[1]) + half_dot(left[1], right[0])
    return (real, imag)


def two_sided(matrix, wave):
    inner = complex_dot(matrix, wave)
    return complex_dot(inner, (matrix[0].T, matrix[1].T))


def tables(phase, patch):
    taps = phase.shape[0]
    rows = jnp.arange(patch, dtype=jnp.int32)[:, None]
    cols = jnp.arange(patch, dtype=jnp.int32)[None, :]
    offset = cols - rows + taps // 2
    picked = (offset[:, :, None] == jnp.arange(taps, dtype=jnp.int32)[None, None, :]).astype(
        phase.dtype
    )
    scale = 1.0 / jnp.sqrt(jnp.asarray(taps, phase.dtype))
    kern_re = (jnp.sum(picked * jnp.cos(phase), axis=-1) * scale).astype(jnp.bfloat16)
    kern_im = (jnp.sum(picked * jnp.sin(phase), axis=-1) * scale).astype(jnp.bfloat16)
    product = rows * cols % patch
    angle = 2.0 * jnp.pi / patch * product.astype(phase.dtype)
    norm = 1.0 / jnp.sqrt(jnp.asarray(patch, phase.dtype))
    dft_re = (jnp.cos(angle) * norm).astype(jnp.bfloat16)
    dft_im = (-jnp.sin(angle) * norm).astype(jnp.bfloat16)
    return ((kern_re, kern_im), (dft_re, dft_im))


def exit_loss(piece_re, piece_im, probe, target, weight, kernel, dft):
    wave_re, wave_im = (probe[0], probe[1])
    slices = piece_re.shape[0]
    for layer in range(slices):
        o_re, o_im = (piece_re[layer], piece_im[layer])
        wave_re, wave_im = (wave_re * o_re - wave_im * o_im, wave_re * o_im + wave_im * o_re)
        if layer + 1 < slices:
            wave_re, wave_im = two_sided(kernel, (wave_re, wave_im))
    far_re, far_im = two_sided(dft, (wave_re, wave_im))
    amplitude = jnp.sqrt(far_re * far_re + far_im * far_im + AMP_FLOOR)
    return 0.5 * weight * jnp.sum((amplitude - target) ** 2)


def local(obj_real, obj_imag, probe, fresnel_phase, row_offset, col_offset, live_count, measured):
    slices, band, width = obj_real.shape
    members = lax.axis_size("pos")
    patch = probe.shape[-1]
    capacity = row_offset.shape[0]
    whole_re, whole_im = (
        lax.all_gather(obj_real, "pos", axis=1, tiled=True),
        lax.all_gather(obj_imag, "pos", axis=1, tiled=True),
    )
    next_re, next_im = from_behind((whole_re, whole_im), "tile", -1)
    ext_re = jnp.concatenate([whole_re, next_re], axis=1)
    ext_im = jnp.concatenate([whole_im, next_im], axis=1)
    rows = whole_re.shape[1]
    kernel, dft = tables(fresnel_phase, patch)
    member = lax.axis_index("pos")
    live = live_count[0]
    zero = jnp.zeros((), jnp.int32)
    grad_many = jax.vmap(
        jax.grad(exit_loss, argnums=(0, 1)), in_axes=(0, 0, None, 0, 0, None, None)
    )

    def cut(field, top, left):
        return lax.dynamic_slice(field, (zero, top, left), (slices, patch, patch))

    slots = member + members * jnp.arange(capacity // members, dtype=jnp.int32)
    tops = jnp.take(row_offset, slots, axis=0)
    lefts = jnp.take(col_offset, slots, axis=0)
    targets = jnp.take(measured, slots, axis=0).astype(jnp.float32)
    weights = (slots < live).astype(jnp.float32)
    pieces_re = jax.vmap(cut, in_axes=(None, 0, 0))(ext_re, tops, lefts)
    pieces_im = jax.vmap(cut, in_axes=(None, 0, 0))(ext_im, tops, lefts)
    grads_re, grads_im = grad_many(pieces_re, pieces_im, probe, targets, weights, kernel, dft)

    def add_one(carry, item):
        top, left, one_re, one_im = item
        acc_re = lax.dynamic_update_slice(
            carry[0], cut(carry[0], top, left) + one_re, (zero, top, left)
        )
        acc_im = lax.dynamic_update_slice(
            carry[1], cut(carry[1], top, left) + one_im, (zero, top, left)
        )
        return ((acc_re, acc_im), None)

    start = (jnp.zeros_like(ext_re), jnp.zeros_like(ext_im))
    (acc_re, acc_im), _ = lax.scan(add_one, start, (tops, lefts, grads_re, grads_im))
    spill_re, spill_im = from_behind((acc_re[:, rows:], acc_im[:, rows:]), "tile", 1)
    out_re, out_im = (
        lax.psum_scatter(acc_re[:, :rows] + spill_re, "pos", scatter_dimension=1, tiled=True),
        lax.psum_scatter(acc_im[:, :rows] + spill_im, "pos", scatter_dimension=1, tiled=True),
    )
    return (out_re, out_im)


def solution(mesh):
    in_specs = (
        P(None, ("tile", "pos"), None),
        P(None, ("tile", "pos"), None),
        P(),
        P(),
        P("tile"),
        P("tile"),
        P("tile"),
        P("tile", None, None),
    )
    out_specs = (P(None, ("tile", "pos"), None), P(None, ("tile", "pos"), None))
    return jax.shard_map(local, mesh=mesh, in_specs=in_specs, out_specs=out_specs, check_vma=False)
```

profile of v0, /device:TPU:6, one launch (start us, length us, event | category | flops | bytes accessed | tf_op | source)
XLA Modules:
  0.0 573.5 jit_solution(6532149877312331927)
XLA Ops:
  12.1 27.2 %all-gather.3.cloned.1.call-done = f32[4,256,256]{2,1,0:T(8,128)} async-done(((f32[4,64,256]{2,1,0:T(8,128)}), f32[4,256,256]{2,1,0:T(8,128)}) %all-gather.3.cloned.1.call-update) | async-done | bytes 1048592 | tf_op jit(solution)/shard_map/all_gather | solution.py:70
  39.3 4.0 collective-permute-start
  46.1 21.9 %all-gather.5.cloned.1.call-done = f32[4,256,256]{2,1,0:T(8,128)} async-done(((f32[4,64,256]{2,1,0:T(8,128)}), f32[4,256,256]{2,1,0:T(8,128)}) %all-gather.5.cloned.1.call-update) | async-done | bytes 1048592 | tf_op jit(solution)/shard_map/all_gather | solution.py:71
  68.0 4.0 collective-permute-start.1
  77.6 59.9 %while.15 = (s32[]{:T(128)}, f32[4,512,256]{2,1,0:T(8,128)}, s32[16,3]{0,1:T(4,128)S(1)}, f32[16,4,128,128]{3,2,0,1:T(8,128)}, s32[]{:T(128)}) while((s32[]{:T(128)}, f32[4,512,256]{2,1,0:T(8,128)}, s32[16,3]{0,1:T(4,128)S(1)}, f32[16,4,128,128]{3,2,0,1:T(8,128)}, s32[]{:T(128)}) %tuple.86), condition=%wide.while_cond, body=%wide.while_body.sunk | while | flops 2 | bytes 525929 | solution.py:86
  93.2 3.1 bitcast_dynamic-update-slice_fusion.4
  96.9 3.1 bitcast_dynamic-update-slice_fusion.4
  100.7 3.1 bitcast_dynamic-update-slice_fusion.4
  108.2 3.1 bitcast_dynamic-update-slice_fusion.4
  123.1 3.1 bitcast_dynamic-update-slice_fusion.4
  134.3 3.1 bitcast_dynamic-update-slice_fusion.4
  142.7 62.0 %while.16 = (s32[]{:T(128)}, f32[4,512,256]{2,1,0:T(8,128)}, s32[16,3]{0,1:T(4,128)S(1)}, f32[16,4,128,128]{3,2,0,1:T(8,128)}, s32[]{:T(128)}) while((s32[]{:T(128)}, f32[4,512,256]{2,1,0:T(8,128)}, s32[16,3]{0,1:T(4,128)S(1)}, f32[16,4,128,128]{3,2,0,1:T(8,128)}, s32[]{:T(128)}) %tuple.100), condition=%wide.while_cond.1, body=%wide.while_body.1.sunk | while | flops 2 | bytes 525929 | solution.py:86
  143.4 3.2 bitcast_dynamic-update-slice_fusion.5
  147.2 3.2 bitcast_dynamic-update-slice_fusion.5
  151.1 3.2 bitcast_dynamic-update-slice_fusion.5
  155.0 3.3 bitcast_dynamic-update-slice_fusion.5
  158.9 3.2 bitcast_dynamic-update-slice_fusion.5
  162.8 3.2 bitcast_dynamic-update-slice_fusion.5
  166.7 3.2 bitcast_dynamic-update-slice_fusion.5
  170.6 3.2 bitcast_dynamic-update-slice_fusion.5
  174.4 3.2 bitcast_dynamic-update-slice_fusion.5
  178.3 3.3 bitcast_dynamic-update-slice_fusion.5
  182.2 3.2 bitcast_dynamic-update-slice_fusion.5
  186.1 3.2 bitcast_dynamic-update-slice_fusion.5
  189.9 3.2 bitcast_dynamic-update-slice_fusion.5
  193.8 3.2 bitcast_dynamic-update-slice_fusion.5
  197.7 3.2 bitcast_dynamic-update-slice_fusion.5
  201.5 3.2 bitcast_dynamic-update-slice_fusion.5
  245.8 246.4 %while.14 = (s32[]{:T(128)}, f32[4,512,256]{2,1,0:T(8,128)}, f32[4,512,256]{2,1,0:T(8,128)}, s32[16]{0:T(128)S(1)}, s32[16]{0:T(128)S(1)}, /*index=5*/f32[16,4,1...) while((s32[]{:T(128)}, f32[4,512,256]{2,1,0:T(8,128)}, ...), condition=%wide.region_3.5_spmd, body=%wide.region_2.4_spmd.sunk | while | flops 131080 | bytes 2621661 | solution.py:108
  252.4 4.4 dynamic_update_slice.9
  256.8 4.3 dynamic_update_slice.8
  267.8 4.4 dynamic_update_slice.9
  272.2 4.3 dynamic_update_slice.8
  283.2 4.4 dynamic_update_slice.9
  287.6 4.4 dynamic_update_slice.8
  298.7 4.3 dynamic_update_slice.9
  303.0 4.3 dynamic_update_slice.8
  314.0 4.4 dynamic_update_slice.9
  318.4 4.4 dynamic_update_slice.8
  329.5 4.4 dynamic_update_slice.9
  333.8 4.4 dynamic_update_slice.8
  344.9 4.4 dynamic_update_slice.9
  349.3 4.3 dynamic_update_slice.8
  360.3 4.4 dynamic_update_slice.9
  364.6 4.3 dynamic_update_slice.8
  375.7 4.3 dynamic_update_slice.9
  380.0 4.3 dynamic_update_slice.8
  391.0 4.4 dynamic_update_slice.9
  395.4 4.4 dynamic_update_slice.8
  406.5 4.4 dynamic_update_slice.9
  410.9 4.4 dynamic_update_slice.8
  421.9 4.4 dynamic_update_slice.9
  426.3 4.4 dynamic_update_slice.8
  437.4 4.4 dynamic_update_slice.9
  441.7 4.4 dynamic_update_slice.8
  452.8 4.4 dynamic_update_slice.9
  457.2 4.3 dynamic_update_slice.8
  468.2 4.3 dynamic_update_slice.9
  472.5 4.3 dynamic_update_slice.8
  483.5 4.4 dynamic_update_slice.9
  487.9 4.3 dynamic_update_slice.8
  495.4 16.3 %collective-permute-done.3 = f32[4,256,256]{2,1,0:T(8,128)S(1)} collective-permute-done((f32[4,256,256]{2,1,0:T(8,128)S(1)}, f32[4,256,256]{2,1,0:T(8,128)S(1)}, u32[]{:S(2)}, u32[]{:S(2)}) %collective-permute-start.3) | collective-permute-done | bytes 1048608 | tf_op jit(solution)/shard_map/ppermute | solution.py:12
  517.6 16.3 %collective-permute-done.2 = f32[4,256,256]{2,1,0:T(8,128)S(1)} collective-permute-done((f32[4,256,256]{2,1,0:T(8,128)S(1)}, f32[4,256,256]{2,1,0:T(8,128)S(1)}, u32[]{:S(2)}, u32[]{:S(2)}) %collective-permute-start.2) | collective-permute-done | bytes 1048608 | tf_op jit(solution)/shard_map/ppermute | solution.py:12
  538.0 29.0 %reduce-scatter.3.cloned.1.call-done = f32[4,64,256]{2,1,0:T(8,128)} async-done(((f32[4,256,256]{2,1,0:T(8,128)}), f32[4,64,256]{2,1,0:T(8,128)}) %reduce-scatter.3.cloned.1.call-update) | async-done | bytes 262160 | tf_op jit(solution)/shard_map/reduce_scatter | solution.py:111
  (242 shorter events, 167.4 us)
Async XLA Ops:
  7.2 36.2 %copy-start = (bf16[64,128,128]{2,1,0:T(8,128)(2,1)S(1)}, bf16[64,128,128]{2,1,0:T(8,128)(2,1)}, u32[]{:S(2)}) copy-start(bf16[64,128,128]{2,1,0:T(8,128)(2,1)} %param.19) | copy-start | bytes 6291460
  7.2 32.1 %all-gather.3.cloned.1.call-start = ((), (), s32[]{:S(2)}) async-start(), calls=%async_computation.2 | async-start | bytes 1310720 | tf_op jit(solution)/shard_map/all_gather | solution.py:70
  7.9 60.1 %all-gather.5.cloned.1.call-start = ((), (), s32[]{:S(2)}) async-start(), calls=%async_computation.3 | async-start | bytes 1310720 | tf_op jit(solution)/shard_map/all_gather | solution.py:71
  8.7 529.3 %reduce-scatter.5.cloned.1.call-start = ((), (), s32[]{:S(2)}) async-start(), calls=%async_computation.5 | async-start | bytes 1310720 | tf_op jit(solution)/shard_map/reduce_scatter | solution.py:112
  39.3 32.8 %collective-permute-start = (f32[4,256,256]{2,1,0:T(8,128)}, f32[4,256,256]{2,1,0:T(8,128)}, u32[]{:S(2)}, u32[]{:S(2)}) collective-permute-start(f32[4,256,256]{2,1,0:T(8,128)} %all-gather.3.cloned.1.call-done), channel_id=1, source_target_pairs={{4,0},{8,4},{12,8},{16,12},{20,16},{24,20},{28,24},{32,28},{36,32}... | collective-permute-start | bytes 3145736 | tf_op jit(solution)/shard_map/ppermute | solution.py:12
  68.0 69.4 %collective-permute-start.1 = (f32[4,256,256]{2,1,0:T(8,128)}, f32[4,256,256]{2,1,0:T(8,128)}, u32[]{:S(2)}, u32[]{:S(2)}) collective-permute-start(f32[4,256,256]{2,1,0:T(8,128)} %all-gather.5.cloned.1.call-done), channel_id=1, source_target_pairs={{4,0},{8,4},{12,8},{16,12},{20,16},{24,20},{28,24},{32,28},{36,32}... | collective-permute-start | bytes 3145736 | tf_op jit(solution)/shard_map/ppermute | solution.py:12
  75.1 62.3 %copy-start.4 = (f32[4,256,256]{2,1,0:T(8,128)S(1)}, f32[4,256,256]{2,1,0:T(8,128)}, u32[]{:S(2)}) copy-start(f32[4,256,256]{2,1,0:T(8,128)} %all-gather.5.cloned.1.call-done) | copy-start | bytes 3145732
  207.2 2.2 copy-start.3
  207.5 3.2 copy-start.2
  493.5 18.2 %collective-permute-start.3 = (f32[4,256,256]{2,1,0:T(8,128)S(1)}, f32[4,256,256]{2,1,0:T(8,128)S(1)}, u32[]{:S(2)}, u32[]{:S(2)}) collective-permute-start(f32[4,256,256]{2,1,0:T(8,128)S(1)} %slice.55), channel_id=1, source_target_pairs={{0,4},{4,8},{8,12},{12,16},{16,20},{20,24},{24,28},{28,32},{32,36}... | collective-permute-start | bytes 3145736 | tf_op jit(solution)/shard_map/ppermute | solution.py:12
  511.7 55.3 %copy-start.1 = (bf16[64,128,128]{2,1,0:T(8,128)(2,1)S(1)}, bf16[64,128,128]{2,1,0:T(8,128)(2,1)}, u32[]{:S(2)}) copy-start(bf16[64,128,128]{2,1,0:T(8,128)(2,1)} %param.19) | copy-start | bytes 6291460
  514.3 52.7 %reduce-scatter.3.cloned.1.call-start = ((), (), s32[]{:S(2)}) async-start(), calls=%async_computation.4 | async-start | bytes 1310720 | tf_op jit(solution)/shard_map/reduce_scatter | solution.py:111
  515.6 18.2 %collective-permute-start.2 = (f32[4,256,256]{2,1,0:T(8,128)S(1)}, f32[4,256,256]{2,1,0:T(8,128)S(1)}, u32[]{:S(2)}, u32[]{:S(2)}) collective-permute-start(f32[4,256,256]{2,1,0:T(8,128)S(1)} %slice.53), channel_id=1, source_target_pairs={{0,4},{4,8},{8,12},{12,16},{16,20},{20,24},{24,28},{28,32},{32,36}... | collective-permute-start | bytes 3145736 | tf_op jit(solution)/shard_map/ppermute | solution.py:12
Sparse Core Ops, SparseCore 0:
  9.8 29.4 all-gather.2
  41.1 26.8 all-gather.4
  514.4 23.5 reduce-scatter.4
  541.1 25.8 reduce-scatter.2
where the time goes:
time: 579 us; the launch traced here: 574 us
  local copies, waits for them, and re-layouts  298 us (51%)
  waiting for transfers between devices  114 us (20%)
  loops' own time  62.4 us (11%)
  other arithmetic  46.4 us (8%)
  matrix products  26 us (4%)
  between operations  15 us (3%)
  starting transfers between devices  12.1 us (2%)
    gather x96, local copies, waits for them, and re-layouts  122 us
    dynamic_update_slice x16, local copies, waits for them, and re-layouts, add_one(): lax.dynamic_update_slice(carry[1], cut(carry[1], top, left) + one_im, (ze...  69.9 us
    dynamic_update_slice x16, local copies, waits for them, and re-layouts, add_one(): lax.dynamic_update_slice(carry[0], cut(carry[0], top, left) + one_re, (ze...  69.8 us
    another operation x1, loops' own time, local(): lax.scan(add_one, start, (tops, lefts, grads_re, grads_im))  62.3 us
    ppermute x4, waiting for transfers between devices, from_behind(): lax.ppermute(value, axis, [(source, source + steps) for source in range(l...  32.6 us
    reduce_scatter x1, waiting for transfers between devices, local(): lax.psum_scatter(acc_re[:, :rows] + spill_re, 'pos', scatter_dimension=1,...  29 us
    all_gather x1, waiting for transfers between devices, local(): lax.all_gather(obj_real, 'pos', axis=1, tiled=True)  27.2 us
    dot_general x64, matrix products, half_dot(): jnp.dot(left.astype(jnp.bfloat16), right.astype(jnp.bfloat16), preferred_...  26 us
  transfers between devices with their start and end apart: 8, of which 6 were waited for; matrix products, arithmetic and copies ran while one was open for 13% of the time, Pallas kernels for 0%

commit v1 on v0

v1 whole, which is shorter than its diff:
```python
import jax
import jax.numpy as jnp
from jax import lax
from jax.experimental import pallas as pl
from jax.experimental.pallas import tpu as pltpu
from jax.sharding import PartitionSpec as P

AMP_FLOOR = 0.25
PATCH = 128
SLICES = 4
SHARD = 64
WINDOW = 3 * SHARD
CAP = 64
GROUP = 2
AXES = ("tile", "pos")


def kernel_table(phase):
    taps = phase.shape[0]
    rows = jnp.arange(PATCH, dtype=jnp.int32)[:, None]
    cols = jnp.arange(PATCH, dtype=jnp.int32)[None, :]
    offset = cols - rows + taps // 2
    picked = (offset[:, :, None] == jnp.arange(taps, dtype=jnp.int32)[None, None, :]).astype(
        phase.dtype
    )
    scale = 1.0 / jnp.sqrt(jnp.asarray(taps, phase.dtype))
    kern_re = (jnp.sum(picked * jnp.cos(phase), axis=-1) * scale).astype(jnp.bfloat16)
    kern_im = (jnp.sum(picked * jnp.sin(phase), axis=-1) * scale).astype(jnp.bfloat16)
    return kern_re, kern_im


def dft_table(dtype):
    rows = jnp.arange(PATCH, dtype=jnp.int32)[:, None]
    cols = jnp.arange(PATCH, dtype=jnp.int32)[None, :]
    product = rows * cols % PATCH
    angle = 2.0 * jnp.pi / PATCH * product.astype(dtype)
    norm = 1.0 / jnp.sqrt(jnp.asarray(PATCH, dtype))
    return (jnp.cos(angle) * norm).astype(jnp.bfloat16), (-jnp.sin(angle) * norm).astype(
        jnp.bfloat16
    )


def left_form(re, im):
    return jnp.block([[re, -im], [im, re]])


def stacked_tables(phase):
    left_k = left_form(*kernel_table(phase))
    left_d = left_form(*dft_table(phase.dtype))
    return jnp.stack([left_k, left_k.T, left_d, left_d.T])


def dot(a, b):
    return jnp.dot(a, b, preferred_element_type=jnp.float32)


def half(x):
    return x.astype(jnp.bfloat16)


def lanes_to_rows(wide):
    re = [wide[j * PATCH : (j + 1) * PATCH, :PATCH] for j in range(GROUP)]
    im = [wide[j * PATCH : (j + 1) * PATCH, PATCH:] for j in range(GROUP)]
    return jnp.concatenate(
        [jnp.concatenate(re, axis=1), jnp.concatenate(im, axis=1)], axis=0
    )


def rows_to_lanes(tall):
    return jnp.concatenate(
        [
            jnp.concatenate(
                [
                    tall[:PATCH, j * PATCH : (j + 1) * PATCH],
                    tall[PATCH:, j * PATCH : (j + 1) * PATCH],
                ],
                axis=1,
            )
            for j in range(GROUP)
        ],
        axis=0,
    )


def body(
    row_ref,
    col_ref,
    place_ref,
    probe_ref,
    table_ref,
    measured_hbm,
    own_hbm,
    via_a_hbm,
    via_b_hbm,
    via_c_hbm,
    send_a_hbm,
    send_b_hbm,
    middle_hbm,
    field,
    total,
    measured,
    wave_save,
    piece_save,
    slots,
    in_sem,
    out_sem,
    measured_sem,
):
    member = place_ref[0]
    live = place_ref[1]
    odd = (member % 2) == 1
    mine = (member + 3) % 4

    def window(ref, third):
        return ref.at[:, :, pl.ds(third * SHARD, SHARD), :]

    load_measured = pltpu.make_async_copy(measured_hbm, measured, measured_sem)
    load_measured.start()
    first = jnp.where(odd, 0, 2)
    load_a = pltpu.make_async_copy(via_a_hbm, window(field, first), in_sem.at[0])
    load_b = pltpu.make_async_copy(via_b_hbm, window(field, 2 - first), in_sem.at[1])
    load_own = pltpu.make_async_copy(own_hbm, window(field, 1), in_sem.at[2])
    load_c = pltpu.make_async_copy(via_c_hbm, window(field, 1), in_sem.at[2])
    load_a.start()
    load_b.start()

    @pl.when(member == 0)
    def _():
        load_c.start()

    @pl.when(member != 0)
    def _():
        load_own.start()

    def list_one(slot, count):
        slots[count] = slot
        hit = jnp.logical_and(slot < live, row_ref[slot] // SHARD == mine)
        return count + hit.astype(jnp.int32)

    count = lax.fori_loop(0, CAP, list_one, jnp.int32(0), unroll=8)
    for spare in range(GROUP):
        slots[count + spare] = 0

    for part in range(2):
        for layer in range(SLICES):
            total[part, layer] = jnp.zeros((WINDOW, 2 * PATCH), jnp.float32)

    load_a.wait()
    load_b.wait()
    load_own.wait()
    load_measured.wait()

    lane = lax.broadcasted_iota(jnp.int32, (1, 8, PATCH), 2)
    sub = lax.broadcasted_iota(jnp.int32, (1, 8, PATCH), 1)
    steps = PATCH // 8

    def cut(part, layer, base, rem, left):
        tall = field[part, layer, pl.ds(base, PATCH + 8), :]
        low = tall[:, :PATCH].reshape(steps + 1, 8, PATCH)
        high = tall[:, PATCH:].reshape(steps + 1, 8, PATCH)
        mixed = jnp.where(lane >= left, low, high)
        mixed = pltpu.roll(mixed, (PATCH - left) % PATCH, axis=2)
        mixed = pltpu.roll(mixed, (8 - rem) % 8, axis=1)
        return jnp.where(sub < 8 - rem, mixed[:-1], mixed[1:]).reshape(PATCH, PATCH)

    def add_back(part, layer, base, rem, left, value):
        value = value.reshape(steps, 8, PATCH)
        value = pltpu.roll(value, rem, axis=1)
        value = pltpu.roll(value, left % PATCH, axis=2)
        zero = jnp.zeros((1, 8, PATCH), jnp.float32)
        above = jnp.concatenate([value, zero], axis=0)
        below = jnp.concatenate([zero, value], axis=0)
        tall = jnp.where(sub >= rem, above, below)
        low = jnp.where(lane >= left, tall, 0.0).reshape(PATCH + 8, PATCH)
        high = jnp.where(lane < left, tall, 0.0).reshape(PATCH + 8, PATCH)
        total[part, layer, pl.ds(base, PATCH + 8), :PATCH] += low
        total[part, layer, pl.ds(base, PATCH + 8), PATCH:] += high

    def group_step(step, carry):
        where = []
        for j in range(GROUP):
            item = step * GROUP + j
            slot = slots[item]
            row = row_ref[slot] % SHARD
            left = col_ref[slot]
            base = pl.multiple_of((row // 8) * 8, 8)
            weight = (item < count).astype(jnp.float32)
            where.append((slot, base, row % 8, left, weight))

        left_k, right_k, left_d, right_d = [table_ref[i] for i in range(4)]
        wide = None
        for layer in range(SLICES):
            res, ims = [], []
            for j in range(GROUP):
                _, base, rem, left, _ = where[j]
                o_re = cut(0, layer, base, rem, left)
                o_im = cut(1, layer, base, rem, left)
                piece_save[0, layer, j] = o_re
                piece_save[1, layer, j] = o_im
                if layer == 0:
                    w_re, w_im = probe_ref[0], probe_ref[1]
                else:
                    w_re = wide[j * PATCH : (j + 1) * PATCH, :PATCH]
                    w_im = wide[j * PATCH : (j + 1) * PATCH, PATCH:]
                res.append(half(w_re * o_re - w_im * o_im))
                ims.append(half(w_re * o_im + w_im * o_re))
            tall = jnp.concatenate(
                [jnp.concatenate(res, axis=1), jnp.concatenate(ims, axis=1)], axis=0
            )
            last = layer + 1 == SLICES
            inner = half(dot(left_d if last else left_k, tall))
            wide = dot(rows_to_lanes(inner), right_d if last else right_k)
            if not last:
                wave_save[layer] = wide

        parts = []
        for j in range(GROUP):
            slot, _, _, _, weight = where[j]
            far_re = wide[j * PATCH : (j + 1) * PATCH, :PATCH]
            far_im = wide[j * PATCH : (j + 1) * PATCH, PATCH:]
            square = far_re * far_re + far_im * far_im + AMP_FLOOR
            target = measured[slot].astype(jnp.float32)
            scale = weight * (1.0 - target * lax.rsqrt(square))
            parts.append(jnp.concatenate([half(far_re * scale), half(far_im * scale)], axis=1))
        back = jnp.concatenate(parts, axis=0)
        for layer in range(SLICES - 1, -1, -1):
            last = layer + 1 == SLICES
            outer = half(dot(back, left_d if last else left_k))
            cot = dot(right_d if last else right_k, lanes_to_rows(outer))
            parts = []
            for j in range(GROUP):
                _, base, rem, left, _ = where[j]
                g_re = cot[:PATCH, j * PATCH : (j + 1) * PATCH]
                g_im = cot[PATCH:, j * PATCH : (j + 1) * PATCH]
                if layer == 0:
                    w_re, w_im = probe_ref[0], probe_ref[1]
                else:
                    w_re = wave_save[layer - 1, j * PATCH : (j + 1) * PATCH, :PATCH]
                    w_im = wave_save[layer - 1, j * PATCH : (j + 1) * PATCH, PATCH:]
                add_back(0, layer, base, rem, left, g_re * w_re + g_im * w_im)
                add_back(1, layer, base, rem, left, g_im * w_re - g_re * w_im)
                if layer > 0:
                    o_re = piece_save[0, layer, j]
                    o_im = piece_save[1, layer, j]
                    parts.append(
                        jnp.concatenate(
                            [half(g_re * o_re + g_im * o_im), half(g_im * o_re - g_re * o_im)],
                            axis=1,
                        )
                    )
            if layer > 0:
                back = jnp.concatenate(parts, axis=0)
        return carry

    lax.fori_loop(0, (count + GROUP - 1) // GROUP, group_step, jnp.int32(0))

    store_a = pltpu.make_async_copy(window(total, first), send_a_hbm, out_sem.at[0])
    store_b = pltpu.make_async_copy(window(total, 2 - first), send_b_hbm, out_sem.at[1])
    store_c = pltpu.make_async_copy(window(total, 1), middle_hbm, out_sem.at[2])
    store_a.start()
    store_b.start()
    store_c.start()
    store_a.wait()
    store_b.wait()
    store_c.wait()


def band_gradient(rows, cols, place, probe, tables, measured, own, via_a, via_b, via_c):
    smem = pl.BlockSpec(memory_space=pltpu.SMEM)
    vmem = pl.BlockSpec(memory_space=pltpu.VMEM)
    hbm = pl.BlockSpec(memory_space=pl.ANY)
    part = jax.ShapeDtypeStruct((2, SLICES, SHARD, 2 * PATCH), jnp.float32)
    whole = (2, SLICES, WINDOW, 2 * PATCH)
    return pl.pallas_call(
        body,
        out_shape=(part, part, part),
        in_specs=[smem, smem, smem, vmem, vmem, hbm, hbm, hbm, hbm, hbm],
        out_specs=(hbm, hbm, hbm),
        scratch_shapes=[
            pltpu.VMEM(whole, jnp.float32),
            pltpu.VMEM(whole, jnp.float32),
            pltpu.VMEM((CAP, PATCH, PATCH), jnp.bfloat16),
            pltpu.VMEM((SLICES - 1, GROUP * PATCH, 2 * PATCH), jnp.float32),
            pltpu.VMEM((2, SLICES, GROUP, PATCH, PATCH), jnp.float32),
            pltpu.SMEM((CAP + GROUP,), jnp.int32),
            pltpu.SemaphoreType.DMA((3,)),
            pltpu.SemaphoreType.DMA((3,)),
            pltpu.SemaphoreType.DMA,
        ],
        compiler_params=pltpu.CompilerParams(vmem_limit_bytes=40 * 1024 * 1024),
        cost_estimate=pl.CostEstimate(
            flops=5_000_000_000, bytes_accessed=8_000_000, transcendentals=0
        ),
    )(rows, cols, place, probe, tables, measured, own, via_a, via_b, via_c)


def route_pairs(tiles):
    via_a, via_b, via_c = [], [], []
    for t in range(tiles):
        at = 4 * t
        via_a += [(at, at + 1), (at + 2, at + 3), (at + 3, at + 2)]
        via_b += [(at + 1, at + 2), (at + 2, at + 1), (at + 3, at)]
        if t > 0:
            via_a.append((at + 1, at - 4))
            via_b.append((at, at - 1))
            via_c.append((at, at - 4))
    return via_a, via_b, via_c


def flipped(pairs):
    return [(b, a) for a, b in pairs]


def local(obj_real, obj_imag, probe, fresnel_phase, row_offset, col_offset, live_count, measured):
    via_a, via_b, via_c = route_pairs(lax.axis_size("tile"))
    own = jnp.stack([obj_real, obj_imag])
    got_c = lax.ppermute(own, AXES, via_c)
    got_a = lax.ppermute(own, AXES, via_a)
    got_b = lax.ppermute(own, AXES, via_b)
    member = lax.axis_index("pos").astype(jnp.int32)
    place = jnp.stack([member, live_count[0]])
    tables = stacked_tables(fresnel_phase)
    send_a, send_b, middle = band_gradient(
        row_offset, col_offset, place, probe, tables, measured, own, got_a, got_b, got_c
    )
    back_c = lax.ppermute(middle, AXES, flipped(via_c))
    back_a = lax.ppermute(send_a, AXES, flipped(via_a))
    back_b = lax.ppermute(send_b, AXES, flipped(via_b))
    out = back_a + back_b + jnp.where(member == 0, back_c, middle)
    return out[0], out[1]


def solution(mesh):
    rows = P(None, AXES, None)
    in_specs = (rows, rows, P(), P(), P("tile"), P("tile"), P("tile"), P("tile", None, None))
    return jax.shard_map(
        local, mesh=mesh, in_specs=in_specs, out_specs=(rows, rows), check_vma=False
    )
```

time: 579 us -> 81.4 us (0.14)
  local copies, waits for them, and re-layouts: 298 us -> 5.08 us
  waiting for transfers between devices: 114 us -> 12.4 us
  loops' own time: 62.4 us -> 0 us
  other arithmetic: 46.4 us -> 9.24 us
  matrix products: 26 us -> 0 us
  Pallas kernels: 0 us -> 25.2 us
  starting transfers between devices: 12.1 us -> 26.6 us
  between operations: 15 us -> 1.48 us
    dynamic_update_slice x32 -> x0, local copies, waits for them, and re-layouts: 140 us -> none  [the longest x16 69.9 us: add_one(): lax.dynamic_update_slice(carry[1], cut(carry[1], top, left) + one_im, (ze...]
    gather x99 -> x0, local copies, waits for them, and re-layouts: 125 us -> none
    another operation x3 -> x0, loops' own time: 62.4 us -> none  [the longest x1 62.3 us: local(): lax.scan(add_one, start, (tops, lefts, grads_re, grads_im))]
    all_gather x2 -> x0, waiting for transfers between devices: 49.1 us -> none  [the longest x1 27.2 us: local(): lax.all_gather(obj_real, 'pos', axis=1, tiled=True)]
    reduce_scatter x2 -> x0, waiting for transfers between devices: 30.8 us -> none  [the longest x1 29 us: local(): lax.psum_scatter(acc_re[:, :rows] + spill_re, 'pos', scatter_dimension=1,...]
    add x19 -> x2, other arithmetic: 30.6 us -> 0.18 us  [the longest x1 0.17 us: local(): out = back_a + back_b + jnp.where(member == 0, back_c, middle)]
    dot_general x64 -> x0, matrix products: 26 us -> none  [half_dot(): jnp.dot(left.astype(jnp.bfloat16), right.astype(jnp.bfloat16), preferred_...]
    pallas_call x0 -> x1, Pallas kernels: none -> 25.2 us  [band_gradient(): pl.pallas_call(body, out_shape=(part, part, part), in_specs=[smem, smem,...]
  transfers between devices with their start and end apart: 8 -> 6, of which waited for: 6 -> 3; matrix products, arithmetic and copies ran while one was open for 13% -> 13% of each run, Pallas kernels for 0% -> 0%
where the time goes in v1:
time: 81.4 us; the launch traced here: 80.1 us
  starting transfers between devices  26.6 us (33%)
  Pallas kernels  25.2 us (31%)
  waiting for transfers between devices  12.4 us (15%)
  other arithmetic  9.24 us (11%)
  local copies, waits for them, and re-layouts  5.08 us (6%)
  between operations  1.48 us (2%)
    pallas_call x1, Pallas kernels, band_gradient(): pl.pallas_call(body, out_shape=(part, part, part), in_specs=[smem, smem,...  25.2 us
    ppermute x1, starting transfers between devices, local(): back_b = lax.ppermute(send_b, AXES, flipped(via_b))  10.3 us
    ppermute x1, waiting for transfers between devices, local(): back_a = lax.ppermute(send_a, AXES, flipped(via_a))  9.19 us
    ppermute x1, starting transfers between devices, local(): got_c = lax.ppermute(own, AXES, via_c)  7.47 us
    another operation x3, other arithmetic, stacked_tables(): return jnp.stack([left_k, left_k.T, left_d, left_d.T])  4.05 us
    ppermute x1, starting transfers between devices, local(): got_b = lax.ppermute(own, AXES, via_b)  3.15 us
    ppermute x1, waiting for transfers between devices, local(): back_c = lax.ppermute(middle, AXES, flipped(via_c))  2.92 us
    ppermute x1, starting transfers between devices, local(): got_a = lax.ppermute(own, AXES, via_a)  1.92 us
  transfers between devices with their start and end apart: 6, of which 3 were waited for; matrix products, arithmetic and copies ran while one was open for 13% of the time, Pallas kernels for 0%

profile of v1, /device:TPU:6, one launch (start us, length us, event | category | flops | bytes accessed | tf_op | source)
XLA Modules:
  0.0 80.1 jit_solution(5081854485254262510)
XLA Ops:
  0.6 0.0 copy-start
  0.6 0.0 copy-start.3
  0.7 0.0 copy-start.4
  0.7 0.0 copy-start.5
  0.7 1.2 %pad_maximum_fusion.1.own_hbm = f32[2,4,64,256]{3,2,1,0:T(8,128)S(1)} fusion(f32[1,4,64,256]{3,2,1,0:T(8,128)} %bitcast.19, f32[1,4,64,256]{3,2,1,0:T(8,128)} %bitcast.20), kind=kLoop, calls=%fused_computation.4 | loop fusion | flops 131072 | bytes 1048576 | tf_op jit(solution)/shard_map/stack | solution.py:316
  1.9 7.5 %collective-permute-start.2 = (f32[2,4,64,256]{3,2,1,0:T(8,128)S(1)}, f32[2,4,64,256]{3,2,1,0:T(8,128)S(1)}, u32[]{:S(2)}, u32[]{:S(2)}) collective-permute-start(f32[2,4,64,256]{3,2,1,0:T(8,128)S(1)} %pad_maximum_fusion.1.own_hbm), channel_id=1, source_target_pairs={{4,0},{8,4},{12,8},{16,12},{20,16},{24,20},{28,24},{32,28},{36,32}... | collective-permute-start | bytes 1572872 | tf_op jit(solution)/shard_map/ppermute | solution.py:317
  9.4 3.1 %collective-permute-start.1 = (f32[2,4,64,256]{3,2,1,0:T(8,128)S(1)}, f32[2,4,64,256]{3,2,1,0:T(8,128)}, u32[]{:S(2)}, u32[]{:S(2)}) collective-permute-start(f32[2,4,64,256]{3,2,1,0:T(8,128)S(1)} %pad_maximum_fusion.1.own_hbm), channel_id=1, source_target_pairs={{1,2},{2,1},{3,0},{5,6},{6,5},{7,4},{4,3},{9,10},{10,9},{11,8},{8,... | collective-permute-start | bytes 1572872 | tf_op jit(solution)/shard_map/ppermute | solution.py:319
  12.5 1.9 %collective-permute-start = (f32[2,4,64,256]{3,2,1,0:T(8,128)S(1)}, f32[2,4,64,256]{3,2,1,0:T(8,128)}, u32[]{:S(2)}, u32[]{:S(2)}) collective-permute-start(f32[2,4,64,256]{3,2,1,0:T(8,128)S(1)} %pad_maximum_fusion.1.own_hbm), channel_id=1, source_target_pairs={{0,1},{2,3},{3,2},{4,5},{6,7},{7,6},{5,0},{8,9},{10,11},{11,10},{9... | collective-permute-start | bytes 1572872 | tf_op jit(solution)/shard_map/ppermute | solution.py:318
  14.5 0.9 %fusion.10 = bf16[128,128]{0,1:T(8,128)(2,1)} fusion(), kind=kLoop, calls=%fused_computation.28 | loop fusion | flops 327680 | bytes 32768 | tf_op jit(solution)/shard_map/neg | solution.py:44
  15.4 0.9 %multiply_convert_fusion = (bf16[128,128]{0,1:T(8,128)(2,1)}, bf16[128,128]{0,1:T(8,128)(2,1)}) fusion(), kind=kLoop, calls=%fused_computation.16 | loop fusion | flops 311296 | bytes 65536 | tf_op jit(solution)/shard_map/convert_element_type | solution.py:38
  16.9 0.7 fusion.12
  17.6 0.4 select_reduce_fusion
  18.1 0.1 copy.13
  18.1 0.6 fusion.11
  18.8 0.7 copy.12
  19.5 1.5 %fusion.7 = (bf16[1,256,256]{1,2,0:T(8,128)(2,1)S(1)}, bf16[1,256,256]{2,1,0:T(8,128)(2,1)}) fusion(bf16[128,128]{0,1:T(8,128)(2,1)} %get-tuple-element.21, bf16[128,128]{0,1:T(8,128)(2,1)} %get-tuple-element.20, bf16[128,128]{0,1:T(8,128)(2,1)} %fusion.10), kind=kLoop, calls=%fused_computation.25 | loop fusion | flops 524288 | bytes 360448 | tf_op jit(solution)/shard_map/stack | solution.py:50
  21.0 0.1 copy.15
  21.1 0.8 %multiply_convert_fusion.3 = bf16[128,128]{0,1:T(8,128)(2,1)S(1)} fusion(f32[128,128]{0,1:T(8,128)} %copy.12), kind=kLoop, calls=%fused_computation.21 | loop fusion | flops 32768 | bytes 98304 | tf_op jit(solution)/shard_map/convert_element_type | solution.py:27
  22.0 1.4 %fusion.9 = (bf16[1,256,256]{1,2,0:T(8,128)(2,1)S(1)}, bf16[1,256,256]{2,1,0:T(8,128)(2,1)}) fusion(bf16[128,128]{0,1:T(8,128)(2,1)S(1)} %multiply_convert_fusion.3, bf16[128,128]{0,1:T(8,128)(2,1)} %get-tuple-element.11, bf16[128,128]{0,1:T(8,128)(2,1)} %get-tuple-element.10), kind=kLoop, calls=%fused_computation.27 | loop fusion | flops 524288 | bytes 360448 | tf_op jit(solution)/shard_map/stack | solution.py:50
  23.4 0.8 copy.14
  24.2 0.1 pad_add_fusion.place_ref
  24.3 1.1 %pad_maximum_fusion.table_ref = bf16[4,256,256]{2,1,0:T(8,128)(2,1)S(1)} fusion(bf16[1,256,256]{2,1,0:T(8,128)(2,1)} %get-tuple-element.17, bf16[1,256,256]{2,1,0:T(8,128)(2,1)S(1)} %copy.15, bf16[1,256,256]{2,1,0:T(8,128)(2,1)} %get-tuple-element.15, bf16[1,256,256]{2,1,0:T(8,128)(2,1)} %copy.14), kind=kLoop, calls=%fused_computation.3 | loop fusion | flops 786432 | bytes 1048576 | tf_op jit(solution)/shard_map/stack | solution.py:50
  25.4 0.0 collective-permute-done.2.via_c_hbm
  25.4 0.0 copy-start.1
  25.4 0.8 %copy-done.1 = f32[2,4,64,256]{3,2,1,0:T(8,128)} copy-done((f32[2,4,64,256]{3,2,1,0:T(8,128)}, f32[2,4,64,256]{3,2,1,0:T(8,128)S(1)}, u32[]{:S(2)}) %copy-start.1) | copy-done | bytes 524312
  26.2 0.0 collective-permute-done.1.via_b_hbm
  26.2 0.0 collective-permute-done.via_a_hbm
  26.2 0.0 copy-done
  26.2 0.0 copy-done.3
  26.2 0.0 copy-done.4
  26.2 0.0 copy-done.5
  26.3 0.0 copy-start.2
  26.3 1.0 %copy-done.2 = f32[2,4,64,256]{3,2,1,0:T(8,128)S(1)} copy-done((f32[2,4,64,256]{3,2,1,0:T(8,128)S(1)}, f32[2,4,64,256]{3,2,1,0:T(8,128)}, u32[]{:S(2)}) %copy-start.2) | copy-done | bytes 524312
  27.3 25.2 %shard_map.95 = (f32[2,4,64,256]{3,2,1,0:T(8,128)}, f32[2,4,64,256]{3,2,1,0:T(8,128)}, f32[2,4,64,256]{3,2,1,0:T(8,128)S(1)}) custom-call(s32[64]{0:T(128)S(1)} %copy-done.4, s32[64]{0:T(128)S(1)} %copy-done.5, s32[2]{0:T(128)S(1)} %pad_add_fusion.place_ref, f32[2,128,128]{2,1,0:T(8,128)S(1)} %copy-done.3, ...), custom_call_target="tpu_custom_call" | custom-call | flops 5000000000 | bytes 8000000 | tf_op jit(solution)/shard_map/pallas_call | solution.py:274
  52.5 1.9 %collective-permute-start.3 = (f32[2,4,64,256]{3,2,1,0:T(8,128)}, f32[2,4,64,256]{3,2,1,0:T(8,128)S(1)}, u32[]{:S(2)}, u32[]{:S(2)}) collective-permute-start(f32[2,4,64,256]{3,2,1,0:T(8,128)} %get-tuple-element.5), channel_id=1, source_target_pairs={{1,0},{3,2},{2,3},{5,4},{7,6},{6,7},{0,5},{9,8},{11,10},{10,11},{4... | collective-permute-start | bytes 1572872 | tf_op jit(solution)/shard_map/ppermute | solution.py:327
  54.4 10.3 %collective-permute-start.4 = (f32[2,4,64,256]{3,2,1,0:T(8,128)}, f32[2,4,64,256]{3,2,1,0:T(8,128)S(1)}, u32[]{:S(2)}, u32[]{:S(2)}) collective-permute-start(f32[2,4,64,256]{3,2,1,0:T(8,128)} %get-tuple-element.6), channel_id=1, source_target_pairs={{2,1},{1,2},{0,3},{6,5},{5,6},{4,7},{3,4},{10,9},{9,10},{8,11},{7,... | collective-permute-start | bytes 1572872 | tf_op jit(solution)/shard_map/ppermute | solution.py:328
  64.7 1.9 %collective-permute-start.5 = (f32[2,4,64,256]{3,2,1,0:T(8,128)S(1)}, f32[2,4,64,256]{3,2,1,0:T(8,128)S(1)}, u32[]{:S(2)}, u32[]{:S(2)}) collective-permute-start(f32[2,4,64,256]{3,2,1,0:T(8,128)S(1)} %get-tuple-element.7), channel_id=1, source_target_pairs={{0,4},{4,8},{8,12},{12,16},{16,20},{20,24},{24,28},{28,32},{32,36}... | collective-permute-start | bytes 1572872 | tf_op jit(solution)/shard_map/ppermute | solution.py:326
  66.6 9.2 %collective-permute-done.3 = f32[2,4,64,256]{3,2,1,0:T(8,128)S(1)} collective-permute-done((f32[2,4,64,256]{3,2,1,0:T(8,128)}, f32[2,4,64,256]{3,2,1,0:T(8,128)S(1)}, u32[]{:S(2)}, u32[]{:S(2)}) %collective-permute-start.3) | collective-permute-done | bytes 524320 | tf_op jit(solution)/shard_map/ppermute | solution.py:327
  75.8 0.3 collective-permute-done.4
  76.1 2.9 %collective-permute-done.5 = f32[2,4,64,256]{3,2,1,0:T(8,128)S(1)} collective-permute-done((f32[2,4,64,256]{3,2,1,0:T(8,128)S(1)}, f32[2,4,64,256]{3,2,1,0:T(8,128)S(1)}, u32[]{:S(2)}, u32[]{:S(2)}) %collective-permute-start.5) | collective-permute-done | bytes 524320 | tf_op jit(solution)/shard_map/ppermute | solution.py:326
  79.0 0.2 select_add_fusion
  79.2 0.8 %slice_bitcast_fusion = (f32[4,64,256]{2,1,0:T(8,128)}, f32[4,64,256]{2,1,0:T(8,128)}) fusion(f32[2,4,64,256]{3,2,1,0:T(8,128)S(1)} %select_add_fusion), kind=kLoop, calls=%fused_computation.6 | loop fusion | bytes 1048576 | tf_op jit(solution)/shard_map/squeeze | solution.py:330
  (1 shorter events, 0.0 us)
Async XLA Ops:
  0.6 25.6 %copy-start = (bf16[64,128,128]{2,1,0:T(8,128)(2,1)S(1)}, bf16[64,128,128]{2,1,0:T(8,128)(2,1)}, u32[]{:S(2)}) copy-start(bf16[64,128,128]{2,1,0:T(8,128)(2,1)} %measured_hbm.1) | copy-start | bytes 6291460
  0.6 25.6 %copy-start.3 = (f32[2,128,128]{2,1,0:T(8,128)S(1)}, f32[2,128,128]{2,1,0:T(8,128)}, u32[]{:S(2)}) copy-start(f32[2,128,128]{2,1,0:T(8,128)} %probe_ref.1) | copy-start | bytes 393220
  0.7 25.6 %copy-start.4 = (s32[64]{0:T(128)S(1)}, s32[64]{0:T(128)}, u32[]{:S(2)}) copy-start(s32[64]{0:T(128)} %row_ref.1) | copy-start | bytes 772
  0.7 25.6 %copy-start.5 = (s32[64]{0:T(128)S(1)}, s32[64]{0:T(128)}, u32[]{:S(2)}) copy-start(s32[64]{0:T(128)} %col_ref.1) | copy-start | bytes 772
  1.9 23.5 %collective-permute-start.2 = (f32[2,4,64,256]{3,2,1,0:T(8,128)S(1)}, f32[2,4,64,256]{3,2,1,0:T(8,128)S(1)}, u32[]{:S(2)}, u32[]{:S(2)}) collective-permute-start(f32[2,4,64,256]{3,2,1,0:T(8,128)S(1)} %pad_maximum_fusion.1.own_hbm), channel_id=1, source_target_pairs={{4,0},{8,4},{12,8},{16,12},{20,16},{24,20},{28,24},{32,28},{36,32}... | collective-permute-start | bytes 1572872 | tf_op jit(solution)/shard_map/ppermute | solution.py:317
  9.4 16.8 %collective-permute-start.1 = (f32[2,4,64,256]{3,2,1,0:T(8,128)S(1)}, f32[2,4,64,256]{3,2,1,0:T(8,128)}, u32[]{:S(2)}, u32[]{:S(2)}) collective-permute-start(f32[2,4,64,256]{3,2,1,0:T(8,128)S(1)} %pad_maximum_fusion.1.own_hbm), channel_id=1, source_target_pairs={{1,2},{2,1},{3,0},{5,6},{6,5},{7,4},{4,3},{9,10},{10,9},{11,8},{8,... | collective-permute-start | bytes 1572872 | tf_op jit(solution)/shard_map/ppermute | solution.py:319
  12.5 13.7 %collective-permute-start = (f32[2,4,64,256]{3,2,1,0:T(8,128)S(1)}, f32[2,4,64,256]{3,2,1,0:T(8,128)}, u32[]{:S(2)}, u32[]{:S(2)}) collective-permute-start(f32[2,4,64,256]{3,2,1,0:T(8,128)S(1)} %pad_maximum_fusion.1.own_hbm), channel_id=1, source_target_pairs={{0,1},{2,3},{3,2},{4,5},{6,7},{7,6},{5,0},{8,9},{10,11},{11,10},{9... | collective-permute-start | bytes 1572872 | tf_op jit(solution)/shard_map/ppermute | solution.py:318
  25.4 0.8 %copy-start.1 = (f32[2,4,64,256]{3,2,1,0:T(8,128)}, f32[2,4,64,256]{3,2,1,0:T(8,128)S(1)}, u32[]{:S(2)}) copy-start(f32[2,4,64,256]{3,2,1,0:T(8,128)S(1)} %collective-permute-done.2.via_c_hbm) | copy-start | bytes 1572868
  26.3 1.0 %copy-start.2 = (f32[2,4,64,256]{3,2,1,0:T(8,128)S(1)}, f32[2,4,64,256]{3,2,1,0:T(8,128)}, u32[]{:S(2)}) copy-start(f32[2,4,64,256]{3,2,1,0:T(8,128)} %copy-done.1) | copy-start | bytes 1572868
  52.5 23.3 %collective-permute-start.3 = (f32[2,4,64,256]{3,2,1,0:T(8,128)}, f32[2,4,64,256]{3,2,1,0:T(8,128)S(1)}, u32[]{:S(2)}, u32[]{:S(2)}) collective-permute-start(f32[2,4,64,256]{3,2,1,0:T(8,128)} %get-tuple-element.5), channel_id=1, source_target_pairs={{1,0},{3,2},{2,3},{5,4},{7,6},{6,7},{0,5},{9,8},{11,10},{10,11},{4... | collective-permute-start | bytes 1572872 | tf_op jit(solution)/shard_map/ppermute | solution.py:327
  54.4 21.7 %collective-permute-start.4 = (f32[2,4,64,256]{3,2,1,0:T(8,128)}, f32[2,4,64,256]{3,2,1,0:T(8,128)S(1)}, u32[]{:S(2)}, u32[]{:S(2)}) collective-permute-start(f32[2,4,64,256]{3,2,1,0:T(8,128)} %get-tuple-element.6), channel_id=1, source_target_pairs={{2,1},{1,2},{0,3},{6,5},{5,6},{4,7},{3,4},{10,9},{9,10},{8,11},{7,... | collective-permute-start | bytes 1572872 | tf_op jit(solution)/shard_map/ppermute | solution.py:328
  64.7 14.3 %collective-permute-start.5 = (f32[2,4,64,256]{3,2,1,0:T(8,128)S(1)}, f32[2,4,64,256]{3,2,1,0:T(8,128)S(1)}, u32[]{:S(2)}, u32[]{:S(2)}) collective-permute-start(f32[2,4,64,256]{3,2,1,0:T(8,128)S(1)} %get-tuple-element.7), channel_id=1, source_target_pairs={{0,4},{4,8},{8,12},{12,16},{16,20},{20,24},{24,28},{28,32},{32,36}... | collective-permute-start | bytes 1572872 | tf_op jit(solution)/shard_map/ppermute | solution.py:326

commit v2 on v1

--- a/solution.py
+++ b/solution.py
@@ -1,5 +1,6 @@
 import jax
 import jax.numpy as jnp
+import numpy as np
 from jax import lax
 from jax.experimental import pallas as pl
 from jax.experimental.pallas import tpu as pltpu
@@ -11,7 +12,8 @@
 SHARD = 64
 WINDOW = 3 * SHARD
 CAP = 64
-GROUP = 2
+GROUP = 8
+TAIL = 4
 AXES = ("tile", "pos")
 
 
@@ -29,25 +31,20 @@
     return kern_re, kern_im
 
 
-def dft_table(dtype):
-    rows = jnp.arange(PATCH, dtype=jnp.int32)[:, None]
-    cols = jnp.arange(PATCH, dtype=jnp.int32)[None, :]
-    product = rows * cols % PATCH
-    angle = 2.0 * jnp.pi / PATCH * product.astype(dtype)
-    norm = 1.0 / jnp.sqrt(jnp.asarray(PATCH, dtype))
-    return (jnp.cos(angle) * norm).astype(jnp.bfloat16), (-jnp.sin(angle) * norm).astype(
-        jnp.bfloat16
-    )
-
-
-def left_form(re, im):
-    return jnp.block([[re, -im], [im, re]])
+def dft_table():
+    index = np.arange(PATCH, dtype=np.int32)
+    product = index[:, None] * index[None, :] % PATCH
+    angle = np.float32(2.0 * np.pi / PATCH) * product.astype(np.float32)
+    norm = np.float32(1.0) / np.sqrt(np.float32(PATCH))
+    return (np.cos(angle) * norm).astype(jnp.bfloat16), (-np.sin(angle) * norm).astype(jnp.bfloat16)
 
 
 def stacked_tables(phase):
-    left_k = left_form(*kernel_table(phase))
-    left_d = left_form(*dft_table(phase.dtype))
-    return jnp.stack([left_k, left_k.T, left_d, left_d.T])
+    re, im = kernel_table(phase)
+    left_k = jnp.block([[re, -im], [im, re]])
+    dft_re, dft_im = dft_table()
+    left_d = np.block([[dft_re, -dft_im], [dft_im, dft_re]])
+    return jnp.stack([left_k, left_k.T]), jnp.asarray(np.stack([left_d, left_d.T]))
 
 
 def dot(a, b):
@@ -58,15 +55,15 @@
     return x.astype(jnp.bfloat16)
 
 
-def lanes_to_rows(wide):
-    re = [wide[j * PATCH : (j + 1) * PATCH, :PATCH] for j in range(GROUP)]
-    im = [wide[j * PATCH : (j + 1) * PATCH, PATCH:] for j in range(GROUP)]
+def lanes_to_rows(wide, size):
+    re = [wide[j * PATCH : (j + 1) * PATCH, :PATCH] for j in range(size)]
+    im = [wide[j * PATCH : (j + 1) * PATCH, PATCH:] for j in range(size)]
     return jnp.concatenate(
         [jnp.concatenate(re, axis=1), jnp.concatenate(im, axis=1)], axis=0
     )
 
 
-def rows_to_lanes(tall):
+def rows_to_lanes(tall, size):
     return jnp.concatenate(
         [
             jnp.concatenate(
@@ -76,7 +73,7 @@
                 ],
                 axis=1,
             )
-            for j in range(GROUP)
+            for j in range(size)
         ],
         axis=0,
     )
@@ -87,7 +84,8 @@
     col_ref,
     place_ref,
     probe_ref,
-    table_ref,
+    prop_ref,
+    dft_ref,
     measured_hbm,
     own_hbm,
     via_a_hbm,
@@ -176,10 +174,10 @@
         total[part, layer, pl.ds(base, PATCH + 8), :PATCH] += low
         total[part, layer, pl.ds(base, PATCH + 8), PATCH:] += high
 
-    def group_step(step, carry):
+    def group(start, size):
         where = []
-        for j in range(GROUP):
-            item = step * GROUP + j
+        for j in range(size):
+            item = start + j
             slot = slots[item]
             row = row_ref[slot] % SHARD
             left = col_ref[slot]
@@ -187,16 +185,18 @@
             weight = (item < count).astype(jnp.float32)
             where.append((slot, base, row % 8, left, weight))
 
-        left_k, right_k, left_d, right_d = [table_ref[i] for i in range(4)]
+        left_k, right_k = prop_ref[0], prop_ref[1]
+        left_d, right_d = dft_ref[0], dft_ref[1]
         wide = None
         for layer in range(SLICES):
             res, ims = [], []
-            for j in range(GROUP):
+            for j in range(size):
                 _, base, rem, left, _ = where[j]
                 o_re = cut(0, layer, base, rem, left)
                 o_im = cut(1, layer, base, rem, left)
-                piece_save[0, layer, j] = o_re
-                piece_save[1, layer, j] = o_im
+                if layer > 0:
+                    piece_save[0, layer - 1, j] = o_re
+                    piece_save[1, layer - 1, j] = o_im
                 if layer == 0:
                     w_re, w_im = probe_ref[0], probe_ref[1]
                 else:
@@ -209,12 +209,12 @@
             )
             last = layer + 1 == SLICES
             inner = half(dot(left_d if last else left_k, tall))
-            wide = dot(rows_to_lanes(inner), right_d if last else right_k)
+            wide = dot(rows_to_lanes(inner, size), right_d if last else right_k)
             if not last:
-                wave_save[layer] = wide
+                wave_save[layer, : size * PATCH] = wide
 
         parts = []
-        for j in range(GROUP):
+        for j in range(size):
             slot, _, _, _, weight = where[j]
             far_re = wide[j * PATCH : (j + 1) * PATCH, :PATCH]
             far_im = wide[j * PATCH : (j + 1) * PATCH, PATCH:]
@@ -226,9 +226,9 @@
         for layer in range(SLICES - 1, -1, -1):
             last = layer + 1 == SLICES
             outer = half(dot(back, left_d if last else left_k))
-            cot = dot(right_d if last else right_k, lanes_to_rows(outer))
+            cot = dot(right_d if last else right_k, lanes_to_rows(outer, size))
             parts = []
-            for j in range(GROUP):
+            for j in range(size):
                 _, base, rem, left, _ = where[j]
                 g_re = cot[:PATCH, j * PATCH : (j + 1) * PATCH]
                 g_im = cot[PATCH:, j * PATCH : (j + 1) * PATCH]
@@ -240,8 +240,8 @@
                 add_back(0, layer, base, rem, left, g_re * w_re + g_im * w_im)
                 add_back(1, layer, base, rem, left, g_im * w_re - g_re * w_im)
                 if layer > 0:
-                    o_re = piece_save[0, layer, j]
-                    o_im = piece_save[1, layer, j]
+                    o_re = piece_save[0, layer - 1, j]
+                    o_im = piece_save[1, layer - 1, j]
                     parts.append(
                         jnp.concatenate(
                             [half(g_re * o_re + g_im * o_im), half(g_im * o_re - g_re * o_im)],
@@ -250,9 +250,18 @@
                     )
             if layer > 0:
                 back = jnp.concatenate(parts, axis=0)
+
+    def full_step(step, carry):
+        group(step * GROUP, GROUP)
         return carry
 
-    lax.fori_loop(0, (count + GROUP - 1) // GROUP, group_step, jnp.int32(0))
+    rest = count % GROUP
+    steps_full = count // GROUP + (rest > TAIL).astype(jnp.int32)
+    lax.fori_loop(0, steps_full, full_step, jnp.int32(0))
+
+    @pl.when(jnp.logical_and(rest > 0, rest <= TAIL))
+    def _():
+        group(steps_full * GROUP, TAIL)
 
     store_a = pltpu.make_async_copy(window(total, first), send_a_hbm, out_sem.at[0])
     store_b = pltpu.make_async_copy(window(total, 2 - first), send_b_hbm, out_sem.at[1])
@@ -268,30 +277,30 @@
 def band_gradient(rows, cols, place, probe, tables, measured, own, via_a, via_b, via_c):
     smem = pl.BlockSpec(memory_space=pltpu.SMEM)
     vmem = pl.BlockSpec(memory_space=pltpu.VMEM)
-    hbm = pl.BlockSpec(memory_space=pl.ANY)
+    hbm = pl.BlockSpec(memory_space=pltpu.HBM)
     part = jax.ShapeDtypeStruct((2, SLICES, SHARD, 2 * PATCH), jnp.float32)
     whole = (2, SLICES, WINDOW, 2 * PATCH)
     return pl.pallas_call(
         body,
         out_shape=(part, part, part),
-        in_specs=[smem, smem, smem, vmem, vmem, hbm, hbm, hbm, hbm, hbm],
+        in_specs=[smem, smem, smem, vmem, vmem, vmem, hbm, hbm, hbm, hbm, hbm],
         out_specs=(hbm, hbm, hbm),
         scratch_shapes=[
             pltpu.VMEM(whole, jnp.float32),
             pltpu.VMEM(whole, jnp.float32),
             pltpu.VMEM((CAP, PATCH, PATCH), jnp.bfloat16),
             pltpu.VMEM((SLICES - 1, GROUP * PATCH, 2 * PATCH), jnp.float32),
-            pltpu.VMEM((2, SLICES, GROUP, PATCH, PATCH), jnp.float32),
+            pltpu.VMEM((2, SLICES - 1, GROUP, PATCH, PATCH), jnp.float32),
             pltpu.SMEM((CAP + GROUP,), jnp.int32),
             pltpu.SemaphoreType.DMA((3,)),
             pltpu.SemaphoreType.DMA((3,)),
             pltpu.SemaphoreType.DMA,
         ],
-        compiler_params=pltpu.CompilerParams(vmem_limit_bytes=40 * 1024 * 1024),
+        compiler_params=pltpu.CompilerParams(vmem_limit_bytes=48 * 1024 * 1024),
         cost_estimate=pl.CostEstimate(
             flops=5_000_000_000, bytes_accessed=8_000_000, transcendentals=0
         ),
-    )(rows, cols, place, probe, tables, measured, own, via_a, via_b, via_c)
+    )(rows, cols, place, probe, *tables, measured, own, via_a, via_b, via_c)
 
 
 def route_pairs(tiles):

time: 81.4 us -> 59.3 us (0.73)
  the two profiles are of different devices: /device:TPU:6 before, /device:TPU:4 now
where the time goes in v2:
time: 59.3 us; the launch traced here: 58.1 us
  waiting for transfers between devices  23.5 us (40%)
  starting transfers between devices  18.5 us (31%)
  Pallas kernels  10.9 us (18%)
  other arithmetic  1.85 us (3%)
  local copies, waits for them, and re-layouts  1.83 us (3%)
  between operations  1.47 us (2%)
    pallas_call x1, Pallas kernels, band_gradient(): pl.pallas_call(body, out_shape=(part, part, part), in_specs=[smem, smem,...  10.9 us
    ppermute x1, waiting for transfers between devices, local(): back_a = lax.ppermute(send_a, AXES, flipped(via_a))  7.47 us
    ppermute x1, starting transfers between devices, local(): got_c = lax.ppermute(own, AXES, via_c)  7.18 us
    ppermute x1, waiting for transfers between devices, local(): back_b = lax.ppermute(send_b, AXES, flipped(via_b))  5.44 us
    ppermute x1, waiting for transfers between devices, local(): got_b = lax.ppermute(own, AXES, via_b)  4.92 us
    ppermute x1, waiting for transfers between devices, local(): got_a = lax.ppermute(own, AXES, via_a)  3.46 us
    ppermute x1, starting transfers between devices, local(): got_b = lax.ppermute(own, AXES, via_b)  3.14 us
    ppermute x1, starting transfers between devices, local(): back_b = lax.ppermute(send_b, AXES, flipped(via_b))  2.45 us
  transfers between devices with their start and end apart: 6, of which 5 were waited for; matrix products, arithmetic and copies ran while one was open for 3% of the time, Pallas kernels for 0%

profile of v2, /device:TPU:4, one launch (start us, length us, event | category | flops | bytes accessed | tf_op | source)
XLA Modules:
  0.0 58.1 jit_solution(7008469860629435918)
XLA Ops:
  0.6 0.0 copy-start.3
  0.6 0.0 copy-start.2
  0.7 0.0 copy-start.1
  0.7 0.0 copy-start
  0.7 1.1 %pad_maximum_fusion.own_hbm = f32[2,4,64,256]{3,2,1,0:T(8,128)S(1)} fusion(f32[1,4,64,256]{3,2,1,0:T(8,128)} %bitcast.13, f32[1,4,64,256]{3,2,1,0:T(8,128)} %bitcast.14), kind=kLoop, calls=%fused_computation.3 | loop fusion | flops 131072 | bytes 1048576 | tf_op jit(solution)/shard_map/stack | solution.py:325
  1.8 7.2 %collective-permute-start.2 = (f32[2,4,64,256]{3,2,1,0:T(8,128)S(1)}, f32[2,4,64,256]{3,2,1,0:T(8,128)S(1)}, u32[]{:S(2)}, u32[]{:S(2)}) collective-permute-start(f32[2,4,64,256]{3,2,1,0:T(8,128)S(1)} %pad_maximum_fusion.own_hbm), channel_id=1, source_target_pairs={{4,0},{8,4},{12,8},{16,12},{20,16},{24,20},{28,24},{32,28},{36,32}... | collective-permute-start | bytes 1572872 | tf_op jit(solution)/shard_map/ppermute | solution.py:326
  9.0 3.1 %collective-permute-start.1 = (f32[2,4,64,256]{3,2,1,0:T(8,128)S(1)}, f32[2,4,64,256]{3,2,1,0:T(8,128)S(1)}, u32[]{:S(2)}, u32[]{:S(2)}) collective-permute-start(f32[2,4,64,256]{3,2,1,0:T(8,128)S(1)} %pad_maximum_fusion.own_hbm), channel_id=1, source_target_pairs={{1,2},{2,1},{3,0},{5,6},{6,5},{7,4},{4,3},{9,10},{10,9},{11,8},{8,... | collective-permute-start | bytes 1572872 | tf_op jit(solution)/shard_map/ppermute | solution.py:328
  12.1 1.9 %collective-permute-start = (f32[2,4,64,256]{3,2,1,0:T(8,128)S(1)}, f32[2,4,64,256]{3,2,1,0:T(8,128)S(1)}, u32[]{:S(2)}, u32[]{:S(2)}) collective-permute-start(f32[2,4,64,256]{3,2,1,0:T(8,128)S(1)} %pad_maximum_fusion.own_hbm), channel_id=1, source_target_pairs={{0,1},{2,3},{3,2},{4,5},{6,7},{7,6},{5,0},{8,9},{10,11},{11,10},{9... | collective-permute-start | bytes 1572872 | tf_op jit(solution)/shard_map/ppermute | solution.py:327
  14.7 0.7 %fusion.3 = (f32[33]{0:T(128)S(1)}, f32[33]{0:T(128)S(1)}) fusion(f32[33]{0:T(128)} %param.12), kind=kLoop, calls=%fused_computation.16 | loop fusion | bytes 396 | tf_op jit(solution)/shard_map/cos | solution.py:29
  15.4 0.4 select_reduce_fusion
  15.9 0.1 copy.13
  16.0 0.1 copy.12
  16.1 0.1 copy.14
  16.2 0.1 pad_add_fusion.place_ref
  16.3 0.0 collective-permute-done.2.via_c_hbm
  16.4 4.9 %collective-permute-done.1.via_b_hbm = f32[2,4,64,256]{3,2,1,0:T(8,128)S(1)} collective-permute-done((f32[2,4,64,256]{3,2,1,0:T(8,128)S(1)}, f32[2,4,64,256]{3,2,1,0:T(8,128)S(1)}, u32[]{:S(2)}, u32[]{:S(2)}) %collective-permute-start.1) | collective-permute-done | bytes 524320 | tf_op jit(solution)/shard_map/ppermute | solution.py:328
  21.3 3.5 %collective-permute-done.via_a_hbm = f32[2,4,64,256]{3,2,1,0:T(8,128)S(1)} collective-permute-done((f32[2,4,64,256]{3,2,1,0:T(8,128)S(1)}, f32[2,4,64,256]{3,2,1,0:T(8,128)S(1)}, u32[]{:S(2)}, u32[]{:S(2)}) %collective-permute-start) | collective-permute-done | bytes 524320 | tf_op jit(solution)/shard_map/ppermute | solution.py:327
  24.7 0.0 copy-done.3
  24.7 0.0 copy-done.2
  24.7 0.0 copy-done.1
  24.8 0.0 copy-done
  24.8 10.9 %shard_map.104 = (f32[2,4,64,256]{3,2,1,0:T(8,128)}, f32[2,4,64,256]{3,2,1,0:T(8,128)S(1)}, f32[2,4,64,256]{3,2,1,0:T(8,128)S(1)}) custom-call(s32[64]{0:T(128)S(1)} %copy-done.1, s32[64]{0:T(128)S(1)} %copy-done.2, s32[2]{0:T(128)S(1)} %pad_add_fusion.place_ref, f32[2,128,128]{2,1,0:T(8,128)S(1)} %copy-done, ...), custom_call_target="tpu_custom_call" | custom-call | flops 5000000000 | bytes 8000000 | tf_op jit(solution)/shard_map/pallas_call | solution.py:283
  35.7 1.9 %collective-permute-start.3 = (f32[2,4,64,256]{3,2,1,0:T(8,128)}, f32[2,4,64,256]{3,2,1,0:T(8,128)S(1)}, u32[]{:S(2)}, u32[]{:S(2)}) collective-permute-start(f32[2,4,64,256]{3,2,1,0:T(8,128)} %get-tuple-element.5), channel_id=1, source_target_pairs={{1,0},{3,2},{2,3},{5,4},{7,6},{6,7},{0,5},{9,8},{11,10},{10,11},{4... | collective-permute-start | bytes 1572872 | tf_op jit(solution)/shard_map/ppermute | solution.py:336
  37.6 2.5 %collective-permute-start.4 = (f32[2,4,64,256]{3,2,1,0:T(8,128)S(1)}, f32[2,4,64,256]{3,2,1,0:T(8,128)S(1)}, u32[]{:S(2)}, u32[]{:S(2)}) collective-permute-start(f32[2,4,64,256]{3,2,1,0:T(8,128)S(1)} %get-tuple-element.6), channel_id=1, source_target_pairs={{2,1},{1,2},{0,3},{6,5},{5,6},{4,7},{3,4},{10,9},{9,10},{8,11},{7,... | collective-permute-start | bytes 1572872 | tf_op jit(solution)/shard_map/ppermute | solution.py:337
  40.1 1.9 %collective-permute-start.5 = (f32[2,4,64,256]{3,2,1,0:T(8,128)S(1)}, f32[2,4,64,256]{3,2,1,0:T(8,128)S(1)}, u32[]{:S(2)}, u32[]{:S(2)}) collective-permute-start(f32[2,4,64,256]{3,2,1,0:T(8,128)S(1)} %get-tuple-element.7), channel_id=1, source_target_pairs={{0,4},{4,8},{8,12},{12,16},{16,20},{20,24},{24,28},{28,32},{32,36}... | collective-permute-start | bytes 1572872 | tf_op jit(solution)/shard_map/ppermute | solution.py:335
  42.0 7.5 %collective-permute-done.3 = f32[2,4,64,256]{3,2,1,0:T(8,128)S(1)} collective-permute-done((f32[2,4,64,256]{3,2,1,0:T(8,128)}, f32[2,4,64,256]{3,2,1,0:T(8,128)S(1)}, u32[]{:S(2)}, u32[]{:S(2)}) %collective-permute-start.3) | collective-permute-done | bytes 524320 | tf_op jit(solution)/shard_map/ppermute | solution.py:336
  49.5 5.4 %collective-permute-done.4 = f32[2,4,64,256]{3,2,1,0:T(8,128)S(1)} collective-permute-done((f32[2,4,64,256]{3,2,1,0:T(8,128)S(1)}, f32[2,4,64,256]{3,2,1,0:T(8,128)S(1)}, u32[]{:S(2)}, u32[]{:S(2)}) %collective-permute-start.4) | collective-permute-done | bytes 524320 | tf_op jit(solution)/shard_map/ppermute | solution.py:337
  54.9 2.2 %collective-permute-done.5 = f32[2,4,64,256]{3,2,1,0:T(8,128)S(1)} collective-permute-done((f32[2,4,64,256]{3,2,1,0:T(8,128)S(1)}, f32[2,4,64,256]{3,2,1,0:T(8,128)S(1)}, u32[]{:S(2)}, u32[]{:S(2)}) %collective-permute-start.5) | collective-permute-done | bytes 524320 | tf_op jit(solution)/shard_map/ppermute | solution.py:335
  57.1 0.1 select_add_fusion
  57.3 0.8 %slice_bitcast_fusion = (f32[4,64,256]{2,1,0:T(8,128)}, f32[4,64,256]{2,1,0:T(8,128)}) fusion(f32[2,4,64,256]{3,2,1,0:T(8,128)S(1)} %select_add_fusion), kind=kLoop, calls=%fused_computation.5 | loop fusion | bytes 1048576 | tf_op jit(solution)/shard_map/squeeze | solution.py:339
  (5 shorter events, 0.1 us)
Async XLA Ops:
  0.6 24.1 %copy-start.3 = (bf16[2,256,256]{2,1,0:T(8,128)(2,1)S(1)}, bf16[2,256,256]{2,1,0:T(8,128)(2,1)}, u32[]{:S(2)}) copy-start(bf16[2,256,256]{2,1,0:T(8,128)(2,1)} %constant.16.clone.dft_ref) | copy-start | bytes 786436
  0.6 24.1 %copy-start.2 = (s32[64]{0:T(128)S(1)}, s32[64]{0:T(128)}, u32[]{:S(2)}) copy-start(s32[64]{0:T(128)} %col_ref.1) | copy-start | bytes 772
  0.7 24.1 %copy-start.1 = (s32[64]{0:T(128)S(1)}, s32[64]{0:T(128)}, u32[]{:S(2)}) copy-start(s32[64]{0:T(128)} %row_ref.1) | copy-start | bytes 772
  0.7 24.1 %copy-start = (f32[2,128,128]{2,1,0:T(8,128)S(1)}, f32[2,128,128]{2,1,0:T(8,128)}, u32[]{:S(2)}) copy-start(f32[2,128,128]{2,1,0:T(8,128)} %probe_ref.1) | copy-start | bytes 393220
  1.8 14.6 %collective-permute-start.2 = (f32[2,4,64,256]{3,2,1,0:T(8,128)S(1)}, f32[2,4,64,256]{3,2,1,0:T(8,128)S(1)}, u32[]{:S(2)}, u32[]{:S(2)}) collective-permute-start(f32[2,4,64,256]{3,2,1,0:T(8,128)S(1)} %pad_maximum_fusion.own_hbm), channel_id=1, source_target_pairs={{4,0},{8,4},{12,8},{16,12},{20,16},{24,20},{28,24},{32,28},{36,32}... | collective-permute-start | bytes 1572872 | tf_op jit(solution)/shard_map/ppermute | solution.py:326
  9.0 12.3 %collective-permute-start.1 = (f32[2,4,64,256]{3,2,1,0:T(8,128)S(1)}, f32[2,4,64,256]{3,2,1,0:T(8,128)S(1)}, u32[]{:S(2)}, u32[]{:S(2)}) collective-permute-start(f32[2,4,64,256]{3,2,1,0:T(8,128)S(1)} %pad_maximum_fusion.own_hbm), channel_id=1, source_target_pairs={{1,2},{2,1},{3,0},{5,6},{6,5},{7,4},{4,3},{9,10},{10,9},{11,8},{8,... | collective-permute-start | bytes 1572872 | tf_op jit(solution)/shard_map/ppermute | solution.py:328
  12.1 12.6 %collective-permute-start = (f32[2,4,64,256]{3,2,1,0:T(8,128)S(1)}, f32[2,4,64,256]{3,2,1,0:T(8,128)S(1)}, u32[]{:S(2)}, u32[]{:S(2)}) collective-permute-start(f32[2,4,64,256]{3,2,1,0:T(8,128)S(1)} %pad_maximum_fusion.own_hbm), channel_id=1, source_target_pairs={{0,1},{2,3},{3,2},{4,5},{6,7},{7,6},{5,0},{8,9},{10,11},{11,10},{9... | collective-permute-start | bytes 1572872 | tf_op jit(solution)/shard_map/ppermute | solution.py:327
  35.7 13.8 %collective-permute-start.3 = (f32[2,4,64,256]{3,2,1,0:T(8,128)}, f32[2,4,64,256]{3,2,1,0:T(8,128)S(1)}, u32[]{:S(2)}, u32[]{:S(2)}) collective-permute-start(f32[2,4,64,256]{3,2,1,0:T(8,128)} %get-tuple-element.5), channel_id=1, source_target_pairs={{1,0},{3,2},{2,3},{5,4},{7,6},{6,7},{0,5},{9,8},{11,10},{10,11},{4... | collective-permute-start | bytes 1572872 | tf_op jit(solution)/shard_map/ppermute | solution.py:336
  37.6 17.3 %collective-permute-start.4 = (f32[2,4,64,256]{3,2,1,0:T(8,128)S(1)}, f32[2,4,64,256]{3,2,1,0:T(8,128)S(1)}, u32[]{:S(2)}, u32[]{:S(2)}) collective-permute-start(f32[2,4,64,256]{3,2,1,0:T(8,128)S(1)} %get-tuple-element.6), channel_id=1, source_target_pairs={{2,1},{1,2},{0,3},{6,5},{5,6},{4,7},{3,4},{10,9},{9,10},{8,11},{7,... | collective-permute-start | bytes 1572872 | tf_op jit(solution)/shard_map/ppermute | solution.py:337
  40.1 17.0 %collective-permute-start.5 = (f32[2,4,64,256]{3,2,1,0:T(8,128)S(1)}, f32[2,4,64,256]{3,2,1,0:T(8,128)S(1)}, u32[]{:S(2)}, u32[]{:S(2)}) collective-permute-start(f32[2,4,64,256]{3,2,1,0:T(8,128)S(1)} %get-tuple-element.7), channel_id=1, source_target_pairs={{0,4},{4,8},{8,12},{12,16},{16,20},{20,24},{24,28},{28,32},{32,36}... | collective-permute-start | bytes 1572872 | tf_op jit(solution)/shard_map/ppermute | solution.py:335
